TPU v7x, 128 devices: a whole 4x4x4 slice. The times are simulated.
128 devices in a mesh: dp: 16 (over x_hi, y, core), ctx: 8 (over x_lo, z).
Axes of the slice: x: 4 (x_hi: 2, x_lo: 2; x = x_hi * 2 + x_lo), y: 4, z: 4, core: 2. Of those that a mesh axis runs over, the one named last changes fastest.
Arguments:
- qkv: bfloat16 [16384, 3, 4096], P(('dp', 'ctx')), may hold values from -6 to 6
- short_filter: float32 [3, 3, 4096], P(None, None, 'ctx'), may hold values from -3 to 3
- inner_filter: float32 [7, 256], P(None, 'ctx'), may hold values from -2 to 2
- out_weight: bfloat16 [4096, 4096], P('dp', 'ctx'), may hold values from -0.09375 to 0.09375
- cotangent: bfloat16 [16384, 4096], P(('dp', 'ctx')), may hold values from -6 to 6
- order: int32 [16, 1024], P('dp'), may hold values from 0 to 1023, each once within a row
- lengths: int32 [16, 8], P('dp'), may hold values from 1 to 512, 1024 in all within a row
Outputs:
- mixed: bfloat16 [16384, 4096], P(('dp', 'ctx'))
- grad_qkv: bfloat16 [16384, 3, 4096], P(('dp', 'ctx'))
- grad_weight: float32 [4096, 4096], P('dp', 'ctx')
- grad_short: float32 [3, 3, 4096], P(None, None, 'ctx')
- grad_inner: float32 [7, 256], P(None, 'ctx')
Inputs may be any that keep to these rules, and one draw needn't show every extreme that they name: `order`: each row is a permutation of the positions of one context. `lengths`: each row sums to 1024; its longest record is exactly 512.
All inputs are finite; a program needn't handle non-finite values.
Results may differ from a plain program's by a relative error of at most 0.017.
Values may be sent and summed in bfloat16 or wider, within the bound.
A program may use at most 128 MiB of HBM per device.

v0:
```python
import jax
import jax.numpy as jnp
from jax import lax
from jax.sharding import PartitionSpec as P
from jax.experimental import pallas as pl
from jax.experimental.pallas import tpu as pltpu

MESH = pl.DeviceIdType.MESH
F32 = jnp.float32
BF16 = jnp.bfloat16
GROUP = 16
L = 1024
CB = 512
HF = 2048
ROWS = 128
PAD = 16
STRIP = 128
A2A = ((0, 2), (1, 2), (1, 1), (1, 3), (0, 1), (0, 3), (1, 0))


def where_am_i():
    j = lax.axis_index("ctx")
    return j, j // 4, lax.rem(j, 4)


def peer(x, z, dx, dz):
    return lax.rem(x + dx, 2) * 4 + lax.rem(z + dz, 4)


def barrier(ids):
    sem = pltpu.get_barrier_semaphore()
    for d in ids:
        pl.semaphore_signal(sem, inc=1, device_id=d, device_id_type=MESH)
    pl.semaphore_wait(sem, len(ids))


def fill_masks(lens_ref, m_ref):
    p = lax.broadcasted_iota(jnp.int32, m_ref.shape, 0) - PAD
    good = (p > 0) & (p < L)
    end = jnp.int32(0)
    for k in range(lens_ref.shape[1]):
        end = end + lens_ref[0, k]
        good = good & (p != end)
    m_ref[...] = jnp.where(good, 1.0, 0.0).astype(F32)


def fill_gather(order_row_ref, out_ref):
    def step(i, c):
        r0 = pl.multiple_of(i * 128, 128)
        p = lax.broadcasted_iota(jnp.int32, (128, L), 0) + r0
        out_ref[pl.ds(r0, 128), :] = jnp.where(p == order_row_ref[...], 1.0, 0.0).astype(BF16)
        return c

    lax.fori_loop(0, L // 128, step, 0)


def down(x, m):
    return pltpu.roll(x, 1, 0) * m


def up(x, m):
    return pltpu.roll(x * m, x.shape[0] - 1, 0)


def taps3(u, m, filt):
    u1 = down(u, m)
    u2 = down(u1, m)
    return filt[0] * u + filt[1] * u1 + filt[2] * u2


def dp_id(h, yy, c):
    return h * 8 + yy * 2 + c


def coords():
    i = lax.axis_index("dp")
    return i, i // 8, lax.rem(i // 2, 4), lax.rem(i, 2)


def strips(rows, step, fn):
    def body(n, carry):
        fn(pl.ds(pl.multiple_of(n * step, step), step))
        return carry

    lax.fori_loop(0, rows // step, body, 0)


def block_kernel(
    qs, cot, wt, order_row, lens, short, inner_g,
    mixed, dugot, gw_out, short_out, inner_out,
    arrived, upos, feats, perm, mask, ypos, y, cotz, w2, inner,
    dysend, dyrecv, dypos, dupos,
    parts, fwd, got1, got2, final, gacc, gall,
    gsib, ggot, gown, gfwd, ggot1, ggot2, gred, gfin,
    a_s, a_r, c_s, c_r, w_s, w_r, r_s, r_r, q_s, q_r, g_s, g_r, v_s, v_r, l_s,
):
    j, x, z = where_am_i()
    i, h, yy, core = coords()
    xb = peer(x, z, 1, 0)
    zul, zdl, zo = lax.rem(z + 1, 4), lax.rem(z + 3, 4), lax.rem(z + 2, 4)
    zu, zd = x * 4 + zul, x * 4 + zdl
    yu, yd, yo = lax.rem(yy + 1, 4), lax.rem(yy + 3, 4), lax.rem(yy + 2, 4)
    up_y, dn_y, sib = dp_id(h, yu, core), dp_id(h, yd, core), dp_id(h, yy, 1 - core)
    over_y, flip = dp_id(h, yo, core), dp_id(1 - h, yy, core)
    barrier(
        [{"ctx": peer(x, z, dx, dz)} for dx, dz in A2A]
        + [{"dp": up_y}, {"dp": dn_y}, {"dp": over_y}, {"dp": sib}, {"dp": flip}]
        + [{"dp": flip, "ctx": xb}]
    )

    def remote(src, dst, sems, n, to, rn=None):
        return pltpu.make_async_remote_copy(
            src, dst, sems[0].at[n], sems[1].at[n if rn is None else rn], device_id=to, device_id_type=MESH
        )

    def send(src, dst, sems, n, to, rn=None):
        c = remote(src, dst, sems, n, to, rn)
        c.start()
        return c

    def cols(k, width):
        return pl.ds(pl.multiple_of(k * width, width), width)

    mine_rows = pl.ds(pl.multiple_of(j * ROWS, ROWS), ROWS)
    a_in = []
    for n, (dx, dz) in enumerate(A2A):
        p = peer(x, z, dx, dz)
        a_in.append(send(qs.at[:, :, cols(p, CB)], arrived.at[:, mine_rows, :], (a_s, a_r), n, {"ctx": p}))
    own_q = pltpu.make_async_copy(qs.at[:, :, cols(j, CB)], arrived.at[:, mine_rows, :], l_s.at[0])
    own_q.start()

    wsem = (w_s, w_r)
    w_mine = w2.at[x, yy * 2 + core]
    w_a = send(wt, w_mine, wsem, 0, {"dp": flip, "ctx": h * 4 + z}, x)
    w_b = remote(wt, w_mine, wsem, 1, {"ctx": h * 4 + z}, x)
    w_l = pltpu.make_async_copy(wt, w_mine, l_s.at[3])

    @pl.when(h != x)
    def _():
        w_b.start()

    @pl.when(h == x)
    def _():
        w_l.start()

    mine_c = cot.at[:, cols(x, HF)]
    own_c = pltpu.make_async_copy(mine_c, cotz.at[x, z], l_s.at[1])
    own_c.start()

    fill_masks(lens, mask)
    fill_gather(order_row, perm)
    upos[pl.ds(0, PAD), :] = jnp.zeros((PAD, 3 * CB), BF16)
    upos[pl.ds(PAD + L, PAD), :] = jnp.zeros((PAD, 3 * CB), BF16)
    feats[:, pl.ds(L, PAD), :] = jnp.zeros((4, PAD, CB), BF16)
    gacc[...] = jnp.zeros_like(gacc)
    dypos[pl.ds(L, 8), :] = jnp.zeros((8, CB), F32)
    group_of = lax.broadcasted_iota(jnp.int32, (CB // GROUP, CB), 1) // GROUP
    spread = jnp.where(group_of == lax.broadcasted_iota(jnp.int32, (CB // GROUP, CB), 0), 1.0, 0.0).astype(F32)
    inner[...] = jnp.dot(inner_g[...], spread, preferred_element_type=F32, precision=lax.Precision.HIGHEST)

    remote(wt, w2.at[1 - x, yy * 2 + core], wsem, 0, {"ctx": xb}, 1 - x).wait_recv()

    @pl.when(h != x)
    def _():
        remote(wt, w_mine, wsem, 0, {"ctx": xb}, x).wait_recv()

    @pl.when(h == x)
    def _():
        w_l.wait()

    def pair(k):
        return w2.at[:, k * 2 + core]

    def again(ref, n, to):
        return send(ref, ref, wsem, n, {"dp": to})

    wy = [again(pair(yy), 2, up_y), again(pair(yy), 3, dn_y)]
    ws = [again(pair(yy), 6, sib)]
    wy[0].wait_recv()
    wy[1].wait_recv()
    wy += [again(w2.at[0, yd * 2 + core], 4, up_y), again(w2.at[1, yu * 2 + core], 5, dn_y)]
    ws += [again(pair(yd), 7, sib), again(pair(yu), 8, sib)]

    own_q.wait()
    for c in a_in:
        c.wait_recv()

    csem = (c_s, c_r)
    over = send(cot.at[:, cols(1 - x, HF)], cotz.at[x, z], csem, 0, {"ctx": xb})
    u_own = send(mine_c, cotz.at[x, z], csem, 1, {"ctx": zu})
    d_own = send(mine_c, cotz.at[x, z], csem, 2, {"ctx": zd})

    def place(a, c):
        upos[pl.ds(PAD, L), cols(a, CB)] = jnp.dot(perm[...], arrived[a], preferred_element_type=F32).astype(BF16)
        return c

    lax.fori_loop(0, 3, place, 0)

    over.wait_recv()
    theirs = cotz.at[1 - x, z]
    u_oth = send(theirs, theirs, csem, 3, {"ctx": zu})
    d_oth = send(theirs, theirs, csem, 4, {"ctx": zd})

    def forward(n, carry):
        c0 = pl.multiple_of(lax.rem(n, CB // 128) * 128, 128)
        cs = pl.ds(c0, 128)
        r0 = pl.multiple_of((n // (CB // 128)) * STRIP, STRIP)
        m = mask[pl.ds(r0 + 8, STRIP + 8), :]
        made = []
        for a in range(3):
            u = upos[pl.ds(r0, STRIP + PAD), pl.ds(a * CB + c0, 128)].astype(F32)[8:]
            made.append(taps3(u, m, [short[t, pl.ds(a, 1), cs] for t in range(3)]))
        q, k, v = made
        zt = k * v
        w = inner[pl.ds(0, 1), cs] * zt
        for t in range(1, 7):
            zt = down(zt, m)
            w = w + inner[pl.ds(t, 1), cs] * zt
        for a, val in enumerate((q, k, v, w)):
            feats[a, pl.ds(r0, STRIP), cs] = val[8:].astype(BF16)
        ypos[pl.ds(r0, STRIP), cs] = (q * w)[8:].astype(BF16)
        return carry

    lax.fori_loop(0, (CB // 128) * (L // STRIP), forward, 0)
    my_y = cols(x, CB)
    y[:, my_y] = lax.dot_general(perm[...], ypos[...], TN, preferred_element_type=F32).astype(BF16)
    y_x = send(y.at[:, my_y], y.at[:, my_y], csem, 7, {"ctx": xb})

    wy[2].wait_recv()
    wy[3].wait_recv()
    ws.append(again(pair(yo), 9, sib))
    for c in ws:
        c.wait_recv()
    own_c.wait()

    def grads_of(zz):
        lhs = cotz[:, zz].reshape(2 * ROWS, HF)
        there = jnp.dot(lhs, w2[1 - x].reshape(HF, CB), preferred_element_type=F32).astype(BF16)
        here = jnp.dot(lhs, w2[x].reshape(HF, CB), preferred_element_type=F32)
        for a in range(2):
            rs = pl.ds(pl.multiple_of(a * 512 + zz * ROWS, ROWS), ROWS)
            dysend[rs, :] = there[a * ROWS : (a + 1) * ROWS]
            dypos[rs, :] = here[a * ROWS : (a + 1) * ROWS]

    def grads_step(n, carry):
        grads_of(lax.rem(z + 1 + 2 * n, 4))
        return carry

    grads_of(z)
    u_own.wait_recv()
    d_own.wait_recv()
    u_oth.wait_recv()
    d_oth.wait_recv()
    on_u = send(cotz.at[0, zdl], cotz.at[0, zdl], csem, 5, {"ctx": zu})
    on_d = send(cotz.at[1, zul], cotz.at[1, zul], csem, 6, {"ctx": zd})
    lax.fori_loop(0, 2, grads_step, 0)
    on_u.wait_recv()
    on_d.wait_recv()
    grads_of(zo)
    d_x = send(dysend, dyrecv, csem, 8, {"ctx": xb})

    y_x.wait_recv()

    def part(n, carry):
        def rows_of(b):
            return w2[b, pl.ds(n * 2, 2)].reshape(512, CB)

        val = lax.dot_general(y[:, pl.ds(0, CB)], rows_of(0), NT, preferred_element_type=F32) + lax.dot_general(
            y[:, pl.ds(CB, CB)], rows_of(1), NT, preferred_element_type=F32
        )
        for a in range(2):
            for zz in range(4):
                r0 = (a * 4 + zz) * ROWS
                parts[lax.rem(zz - z + 4, 4), a, :, cols(n, 512)] = val[r0 : r0 + ROWS].astype(BF16)
        return carry

    lax.fori_loop(0, HF // 512, part, 0)
    rsem = (r_s, r_r)
    s_u = send(parts.at[2, 0], got1.at[0], rsem, 0, {"ctx": zu})
    s_d = send(parts.at[2, 1], got1.at[1], rsem, 1, {"ctx": zd})

    vsem = (v_s, v_r)

    def weights(which, dst):
        def step(k, carry):
            lhs = cotz[:, :, :, cols(k * 2 + which, 256)].reshape(L, 256)
            val = lax.dot_general(lhs, y[...], TN, preferred_element_type=F32).astype(BF16)
            dst[k, 0] = val[:, :CB]
            dst[k, 1] = val[:, CB:]
            return carry

        lax.fori_loop(0, 4, step, 0)

    weights(1 - core, gsib)
    g_sib = send(gsib, ggot, vsem, 0, {"dp": sib})
    t_u = send(parts.at[1, 1], got2.at[0, 1], rsem, 2, {"ctx": zu})
    t_d = send(parts.at[3, 0], got2.at[1, 0], rsem, 3, {"ctx": zd})
    weights(core, gown)

    def combine(a, k):
        def fn(rs):
            fwd[a, rs, :] = (parts[k, a, rs, :].astype(F32) + got1[a, rs, :].astype(F32)).astype(BF16)

        strips(ROWS, 16, fn)

    s_u.wait_recv()
    combine(0, 1)
    f_u = send(fwd.at[0], got2.at[0, 0], rsem, 4, {"ctx": zu})
    s_d.wait_recv()
    combine(1, 3)
    f_d = send(fwd.at[1], got2.at[1, 1], rsem, 5, {"ctx": zd})

    g_sib.wait_recv()

    def add_pairs(n, carry):
        k, b = n // 2, lax.rem(n, 2)

        def fn(rs):
            gown[k, b, rs, :] = (gown[k, b, rs, :].astype(F32) + ggot[k, b, rs, :].astype(F32)).astype(BF16)

        strips(256, 64, fn)
        return carry

    lax.fori_loop(0, 8, add_pairs, 0)
    gy = [
        send(gown.at[yo, 0], ggot1.at[0], vsem, 1, {"dp": up_y}),
        send(gown.at[yo, 1], ggot1.at[1], vsem, 2, {"dp": dn_y}),
        send(gown.at[yu, 1], ggot2.at[0, 1], vsem, 3, {"dp": up_y}),
        send(gown.at[yd, 0], ggot2.at[1, 0], vsem, 4, {"dp": dn_y}),
    ]

    d_x.wait_recv()

    def add_dy(rs):
        ypos[rs, :] = (dypos[rs, :] + dyrecv[rs, :].astype(F32)).astype(BF16)

    strips(L, 64, add_dy)
    dypos[pl.ds(0, L), :] = jnp.dot(perm[...], ypos[...], preferred_element_type=F32)

    a_out = []
    for c in range(2):

        def backward(n, carry):
            h0 = pl.multiple_of(lax.rem(n, 2) * 128, 128)
            cs = pl.ds(pl.multiple_of(c * 256 + h0, 128), 128)
            r0 = pl.multiple_of((n // 2) * STRIP, STRIP)
            m = mask[pl.ds(r0 + PAD, STRIP + 8), :]
            q, k, v, w = [feats[a, pl.ds(r0, STRIP + PAD), cs].astype(F32)[: STRIP + 8] for a in range(4)]
            dy = dypos[pl.ds(r0, STRIP + 8), cs]

            def total(val):
                return jnp.sum(val.reshape(STRIP // 8, 8, 128), axis=0)

            b = dy * q
            zs = (k * v)[:STRIP]
            dz = inner[pl.ds(0, 1), cs] * b
            gacc[9, :, cs] += total(b[:STRIP] * zs)
            for t in range(1, 7):
                b = up(b, m)
                dz = dz + inner[pl.ds(t, 1), cs] * b
                gacc[9 + t, :, cs] += total(b[:STRIP] * zs)
            df = (dy * w, dz * v, dz * k)
            for a in range(3):
                u = upos[pl.ds(PAD + r0, STRIP), pl.ds(pl.multiple_of(a * CB + c * 256 + h0, 128), 128)].astype(F32)
                b = df[a]
                du = short[0, pl.ds(a, 1), cs] * b
                gacc[a, :, cs] += total(b[:STRIP] * u)
                for t in range(1, 3):
                    b = up(b, m)
                    du = du + short[t, pl.ds(a, 1), cs] * b
                    gacc[t * 3 + a, :, cs] += total(b[:STRIP] * u)
                dupos[pl.ds(r0, STRIP), pl.ds(pl.multiple_of(a * 256 + h0, 128), 128)] = du[:STRIP].astype(BF16)
            return carry

        lax.fori_loop(0, 2 * (L // STRIP), backward, 0)
        val = lax.dot_general(perm[...], dupos[...], TN, preferred_element_type=F32).astype(BF16)
        part_c = pl.ds(c * 256, 256)
        for a in range(3):
            arrived[a, :, part_c] = val[:, a * 256 : (a + 1) * 256]
        there = dugot.at[:, :, pl.ds(pl.multiple_of(j * CB + c * 256, 256), 256)]
        for n, (dx, dz_) in enumerate(A2A):
            p = peer(x, z, dx, dz_)
            rs = pl.ds(pl.multiple_of(p * ROWS, ROWS), ROWS)
            a_out.append(send(arrived.at[:, rs, part_c], there, (q_s, q_r), c * 7 + n, {"ctx": p}))
        lc = pltpu.make_async_copy(arrived.at[:, mine_rows, part_c], there, l_s.at[4 + c])
        lc.start()
        a_out.append(lc)
        if c == 0:
            gy[0].wait_recv()
            gy[1].wait_recv()
            for a, k in ((0, yu), (1, yd)):

                def add_fwd(rs):
                    gfwd[a, rs, :] = (gown[k, a, rs, :].astype(F32) + ggot1[a, rs, :].astype(F32)).astype(BF16)

                strips(256, 64, add_fwd)
            gy.append(send(gfwd.at[0], ggot2.at[0, 0], vsem, 5, {"dp": up_y}))
            gy.append(send(gfwd.at[1], ggot2.at[1, 1], vsem, 6, {"dp": dn_y}))

    for k in range(16):
        gall[0, pl.ds(k, 1), :] = jnp.sum(gacc[k], axis=0, keepdims=True)
    near_y = dp_id(h, yy + 1 - 2 * lax.rem(yy, 2), core)
    gx = []

    def exchange(n):
        gx.append(send(gall.at[2 * n], gall.at[2 * n + 1], (g_s, g_r), n, {"dp": (sib, near_y, over_y, flip)[n]}))

    def summed(n):
        gx[n].wait_recv()
        gall[2 * n + 2] = gall[2 * n] + gall[2 * n + 1]

    exchange(0)

    for cp in (t_u, t_d, f_u, f_d):
        cp.wait_recv()

    def finish(a, dst):
        def fn(rs):
            final[dst, rs, :] = (
                parts[0, a, rs, :].astype(F32) + (got2[0, a, rs, :].astype(F32) + got2[1, a, rs, :].astype(F32))
            ).astype(BF16)

        strips(ROWS, 16, fn)

    finish(1 - x, 0)
    m_x = send(final.at[0], mixed.at[:, cols(x, HF)], rsem, 6, {"ctx": xb})
    summed(0)
    exchange(1)
    finish(x, 1)
    m_own = pltpu.make_async_copy(final.at[1], mixed.at[:, cols(x, HF)], l_s.at[2])
    m_own.start()

    for k in range(2, 6):
        gy[k].wait_recv()
    for a in range(2):

        def add_all(rs):
            gred[a, rs, :] = (
                gown[yy, a, rs, :].astype(F32) + (ggot2[0, a, rs, :].astype(F32) + ggot2[1, a, rs, :].astype(F32))
            ).astype(BF16)

        strips(256, 64, add_all)

    def owner_copy(a):
        return remote(gred.at[a], gfin.at[h], vsem, 7 + a, {"dp": dp_id(x, yy, core), "ctx": a * 4 + z}, 7 + h)

    for a in range(2):

        @pl.when((h != x) | (x != a))
        def _():
            owner_copy(a).start()

    @pl.when(h == x)
    def _():
        def keep(rs):
            gfin[h, rs, :] = gred[x, rs, :]

        strips(256, 64, keep)

    summed(1)
    exchange(2)
    summed(2)
    exchange(3)
    summed(3)
    sums = gall[8]
    for t in range(3):
        short_out[t] = sums[t * 3 : t * 3 + 3]
    inner_out[...] = lax.dot_general(
        sums[9:16], spread, NT, preferred_element_type=F32, precision=lax.Precision.HIGHEST
    )

    for s in range(2):

        @pl.when((h != x) | (h != s))
        def _():
            remote(gred.at[0], gfin.at[s], vsem, 7, {"ctx": xb}, 7 + s).wait_recv()

    def last(rs):
        gw_out[rs, :] = gfin[0, rs, :].astype(F32) + gfin[1, rs, :].astype(F32)

    strips(256, 64, last)

    for a in range(2):

        @pl.when((h != x) | (x != a))
        def _():
            owner_copy(a).wait_send()

    @pl.when(h != x)
    def _():
        w_b.wait_send()

    m_own.wait()
    m_x.wait()
    for cp in (w_a, *wy, *ws, *a_in, over, u_own, d_own, u_oth, d_oth, on_u, on_d, y_x, d_x):
        cp.wait_send()
    for cp in (s_u, s_d, t_u, t_d, f_u, f_d, g_sib, *gy, *gx):
        cp.wait_send()
    for cp in a_out:
        cp.wait()


VM = pl.BlockSpec(memory_space=pltpu.VMEM)
SM = pl.BlockSpec(memory_space=pltpu.SMEM)
HB = pl.BlockSpec(memory_space=pl.ANY)
DMA = pltpu.SemaphoreType.DMA
NT = (((1,), (1,)), ((), ()))
TN = (((0,), (0,)), ((), ()))


def sems(*counts):
    return [DMA((n,)) for n in counts for _ in range(2)]


def block(qs, cot, wt, order_row, lens, short, inner):
    sds = jax.ShapeDtypeStruct
    vm = pltpu.VMEM
    return pl.pallas_call(
        block_kernel,
        out_shape=(
            sds((ROWS, 2 * HF), BF16),
            sds((3, ROWS, 8 * CB), BF16),
            sds((256, CB), F32),
            sds((3, 3, CB), F32),
            sds((7, CB // GROUP), F32),
        ),
        in_specs=[HB, HB, HB, VM, SM, VM, VM],
        out_specs=(HB, HB, VM, VM, VM),
        scratch_shapes=[
            vm((3, L, CB), BF16),
            vm((L + 2 * PAD, 3 * CB), BF16),
            vm((4, L + PAD, CB), BF16),
            vm((L, L), BF16),
            vm((L + 2 * PAD, 128), F32),
            vm((L, CB), BF16),
            vm((L, 2 * CB), BF16),
            vm((2, 4, ROWS, HF), BF16),
            vm((2, 8, 256, CB), BF16),
            vm((7, CB), F32),
            vm((L, CB), BF16),
            vm((L, CB), BF16),
            vm((L + 8, CB), F32),
            vm((L, 768), BF16),
            vm((4, 2, ROWS, HF), BF16),
            vm((2, ROWS, HF), BF16),
            vm((2, ROWS, HF), BF16),
            vm((2, 2, ROWS, HF), BF16),
            vm((2, ROWS, HF), BF16),
            vm((16, 8, CB), F32),
            vm((9, 16, CB), F32),
            vm((4, 2, 256, CB), BF16),
            vm((4, 2, 256, CB), BF16),
            vm((4, 2, 256, CB), BF16),
            vm((2, 256, CB), BF16),
            vm((2, 256, CB), BF16),
            vm((2, 2, 256, CB), BF16),
            vm((2, 256, CB), BF16),
            vm((2, 256, CB), BF16),
            *sems(7, 9, 10, 7, 14, 4, 9),
            DMA((6,)),
        ],
        compiler_params=pltpu.CompilerParams(collective_id=0, has_side_effects=True, vmem_limit_bytes=60 << 20),
        cost_estimate=pl.CostEstimate(flops=30 << 30, bytes_accessed=100 << 20, transcendentals=0),
        name="block",
    )(qs, cot, wt, order_row, lens, short, inner)


def on_device(qkv, short_filter, inner_filter, out_weight, cotangent, order, lengths):
    qs = qkv.transpose(1, 0, 2)
    mixed, dugot, gw, grad_short, grad_inner = block(
        qs, cotangent, out_weight, order, lengths, short_filter, inner_filter
    )
    return (mixed, dugot.transpose(1, 0, 2), gw, grad_short, grad_inner)


def solution(mesh):
    in_specs = (
        P(("dp", "ctx"), None, None),
        P(None, None, "ctx"),
        P(None, "ctx"),
        P("dp", "ctx"),
        P(("dp", "ctx"), None),
        P("dp", None),
        P("dp", None),
    )
    out_specs = (
        P(("dp", "ctx"), None),
        P(("dp", "ctx"), None, None),
        P("dp", "ctx"),
        P(None, None, "ctx"),
        P(None, "ctx"),
    )
    return jax.shard_map(on_device, mesh=mesh, in_specs=in_specs, out_specs=out_specs, check_vma=False)
```

profile of v0, /device:TPU:0, one launch (start us, length us, event | category | flops | bytes accessed | tf_op | source)
XLA Modules:
  0.0 196.3 jit_solution(12015012501493608217)
XLA Ops:
  0.6 187.4 %block.1 = (bf16[128,4096]{1,0:T(8,128)(2,1)}, bf16[3,128,4096]{2,1,0:T(8,128)(2,1)}, f32[256,512]{1,0:T(8,128)}, f32[3,3,512]{2,1,0:T(4,128)}, f32[7,32]{1,0:T(8,128)}) custom-call(bf16[3,128,4096]{2,1,0:T(8,128)(2,1)} %bitcast.3, bf16[128,4096]{1,0:T(8,128)(2,1)} %cot.1, bf16[256,512]{1,0:T(8,128)(2,1)} %wt.1, s32[1,1024]{1,0:T(1,128)} %order_row.1, ...), custom_call_target="tpu_custom_call" | custom-call | flops 32212254720 | bytes 104857600 | tf_op jit(solution)/shard_map/block/pallas_call | solution.py:518
  188.1 2.3 %copy.17 = bf16[128,4096]{1,0:T(8,128)(2,1)} copy(bf16[128,4096]{1,0:T(8,128)(2,1)} %get-tuple-element.20) | data formatting | bytes 2097152
  190.4 0.0 copy-start
  190.4 0.0 copy-start.1
  190.4 0.0 copy-start.2
  190.4 4.0 %copy.18 = bf16[128,3,4096]{2,0,1:T(8,128)(2,1)} copy(bf16[128,3,4096]{2,0,1:T(8,128)(2,1)} %bitcast.2) | data formatting | bytes 6291456
  194.3 0.0 copy-done
  194.3 0.8 copy.19
  195.1 0.0 copy-done.1
  195.1 0.6 copy.20
  195.7 0.0 copy-done.2
  195.7 0.6 copy.21
Async XLA Ops:
  190.4 4.0 %copy-start = (f32[256,512]{1,0:T(8,128)S(1)}, f32[256,512]{1,0:T(8,128)}, u32[]{:S(2)}) copy-start(f32[256,512]{1,0:T(8,128)} %get-tuple-element.22) | copy-start | bytes 1572868
  190.4 4.8 %copy-start.1 = (f32[3,3,512]{2,1,0:T(4,128)S(1)}, f32[3,3,512]{2,1,0:T(4,128)}, u32[]{:S(2)}) copy-start(f32[3,3,512]{2,1,0:T(4,128)} %get-tuple-element.23) | copy-start | bytes 55300
  190.4 5.4 %copy-start.2 = (f32[7,32]{1,0:T(8,128)S(1)}, f32[7,32]{1,0:T(8,128)}, u32[]{:S(2)}) copy-start(f32[7,32]{1,0:T(8,128)} %get-tuple-element.24) | copy-start | bytes 2692
where the time goes:
time: 197 us; the launch traced here: 196 us
  Pallas kernels  187 us (95%)
  local copies, waits for them, and re-layouts  8.26 us (4%)
    pallas_call x1, Pallas kernels, block(): pl.pallas_call(block_kernel, out_shape=(sds((ROWS, 2 * HF), BF16), sds((3...  187 us
    unnamed x11, local copies, waits for them, and re-layouts  8.26 us

commit v1 on v0

--- a/solution.py
+++ b/solution.py
@@ -92,7 +92,7 @@
     dysend, dyrecv, dypos, dupos,
     parts, fwd, got1, got2, final, gacc, gall,
     gsib, ggot, gown, gfwd, ggot1, ggot2, gred, gfin,
-    a_s, a_r, c_s, c_r, w_s, w_r, r_s, r_r, q_s, q_r, g_s, g_r, v_s, v_r, l_s,
+    a_s, a_r, c_s, c_r, w_s, w_r, r_s, r_r, q_s, q_r, g_s, g_r, v_s, v_r, d_s, d_r, l_s,
 ):
     j, x, z = where_am_i()
     i, h, yy, core = coords()
@@ -121,14 +121,6 @@
     def cols(k, width):
         return pl.ds(pl.multiple_of(k * width, width), width)
 
-    mine_rows = pl.ds(pl.multiple_of(j * ROWS, ROWS), ROWS)
-    a_in = []
-    for n, (dx, dz) in enumerate(A2A):
-        p = peer(x, z, dx, dz)
-        a_in.append(send(qs.at[:, :, cols(p, CB)], arrived.at[:, mine_rows, :], (a_s, a_r), n, {"ctx": p}))
-    own_q = pltpu.make_async_copy(qs.at[:, :, cols(j, CB)], arrived.at[:, mine_rows, :], l_s.at[0])
-    own_q.start()
-
     wsem = (w_s, w_r)
     w_mine = w2.at[x, yy * 2 + core]
     w_a = send(wt, w_mine, wsem, 0, {"dp": flip, "ctx": h * 4 + z}, x)
@@ -143,6 +135,23 @@
     def _():
         w_l.start()
 
+    mine_rows = pl.ds(pl.multiple_of(j * ROWS, ROWS), ROWS)
+
+    def streams_in(half):
+        made = []
+        here = arrived.at[:, mine_rows, pl.ds(half * 256, 256)]
+
+        def block_of(p):
+            return qs.at[:, :, pl.ds(pl.multiple_of(p * CB + half * 256, 256), 256)]
+
+        for n, (dx, dz) in enumerate(A2A):
+            p = peer(x, z, dx, dz)
+            made.append(send(block_of(p), here, (a_s, a_r), half * 7 + n, {"ctx": p}))
+        own = pltpu.make_async_copy(block_of(j), here, l_s.at[(0, 8)[half]])
+        own.start()
+        return made, own
+
+    a_in, own_q = streams_in(0)
     mine_c = cot.at[:, cols(x, HF)]
     own_c = pltpu.make_async_copy(mine_c, cotz.at[x, z], l_s.at[1])
     own_c.start()
@@ -176,55 +185,68 @@
 
     wy = [again(pair(yy), 2, up_y), again(pair(yy), 3, dn_y)]
     ws = [again(pair(yy), 6, sib)]
+    later, later_q = streams_in(1)
+
+    def filters(half):
+        def place(a, c):
+            upos[pl.ds(PAD, L), pl.ds(pl.multiple_of(a * CB + half * 256, 256), 256)] = jnp.dot(
+                perm[...], arrived[a, :, pl.ds(half * 256, 256)], preferred_element_type=F32
+            ).astype(BF16)
+            return c
+
+        lax.fori_loop(0, 3, place, 0)
+
+        def forward(n, carry):
+            c0 = pl.multiple_of(half * 256 + lax.rem(n, 2) * 128, 128)
+            cs = pl.ds(c0, 128)
+            r0 = pl.multiple_of((n // 2) * STRIP, STRIP)
+            m = mask[pl.ds(r0 + 8, STRIP + 8), :]
+            made = []
+            for a in range(3):
+                u = upos[pl.ds(r0, STRIP + PAD), pl.ds(a * CB + c0, 128)].astype(F32)[8:]
+                made.append(taps3(u, m, [short[t, pl.ds(a, 1), cs] for t in range(3)]))
+            q, k, v = made
+            zt = k * v
+            w = inner[pl.ds(0, 1), cs] * zt
+            for t in range(1, 7):
+                zt = down(zt, m)
+                w = w + inner[pl.ds(t, 1), cs] * zt
+            for a, val in enumerate((q, k, v, w)):
+                feats[a, pl.ds(r0, STRIP), cs] = val[8:].astype(BF16)
+            ypos[pl.ds(r0, STRIP), cs] = (q * w)[8:].astype(BF16)
+            return carry
+
+        lax.fori_loop(0, 2 * (L // STRIP), forward, 0)
+        my_y = pl.ds(pl.multiple_of(x * CB + half * 256, 256), 256)
+        y[:, my_y] = lax.dot_general(
+            perm[...], ypos[:, pl.ds(half * 256, 256)], TN, preferred_element_type=F32
+        ).astype(BF16)
+        return send(y.at[:, my_y], y.at[:, my_y], csem, 7 + half, {"ctx": xb})
+
+    csem = (c_s, c_r)
+    own_q.wait()
+    for c in a_in:
+        c.wait_recv()
+    y_x = [filters(0)]
+
     wy[0].wait_recv()
     wy[1].wait_recv()
     wy += [again(w2.at[0, yd * 2 + core], 4, up_y), again(w2.at[1, yu * 2 + core], 5, dn_y)]
     ws += [again(pair(yd), 7, sib), again(pair(yu), 8, sib)]
 
-    own_q.wait()
-    for c in a_in:
+    later_q.wait()
+    for c in later:
         c.wait_recv()
-
-    csem = (c_s, c_r)
+    a_in += later
     over = send(cot.at[:, cols(1 - x, HF)], cotz.at[x, z], csem, 0, {"ctx": xb})
     u_own = send(mine_c, cotz.at[x, z], csem, 1, {"ctx": zu})
     d_own = send(mine_c, cotz.at[x, z], csem, 2, {"ctx": zd})
-
-    def place(a, c):
-        upos[pl.ds(PAD, L), cols(a, CB)] = jnp.dot(perm[...], arrived[a], preferred_element_type=F32).astype(BF16)
-        return c
-
-    lax.fori_loop(0, 3, place, 0)
+    y_x.append(filters(1))
 
     over.wait_recv()
     theirs = cotz.at[1 - x, z]
     u_oth = send(theirs, theirs, csem, 3, {"ctx": zu})
     d_oth = send(theirs, theirs, csem, 4, {"ctx": zd})
-
-    def forward(n, carry):
-        c0 = pl.multiple_of(lax.rem(n, CB // 128) * 128, 128)
-        cs = pl.ds(c0, 128)
-        r0 = pl.multiple_of((n // (CB // 128)) * STRIP, STRIP)
-        m = mask[pl.ds(r0 + 8, STRIP + 8), :]
-        made = []
-        for a in range(3):
-            u = upos[pl.ds(r0, STRIP + PAD), pl.ds(a * CB + c0, 128)].astype(F32)[8:]
-            made.append(taps3(u, m, [short[t, pl.ds(a, 1), cs] for t in range(3)]))
-        q, k, v = made
-        zt = k * v
-        w = inner[pl.ds(0, 1), cs] * zt
-        for t in range(1, 7):
-            zt = down(zt, m)
-            w = w + inner[pl.ds(t, 1), cs] * zt
-        for a, val in enumerate((q, k, v, w)):
-            feats[a, pl.ds(r0, STRIP), cs] = val[8:].astype(BF16)
-        ypos[pl.ds(r0, STRIP), cs] = (q * w)[8:].astype(BF16)
-        return carry
-
-    lax.fori_loop(0, (CB // 128) * (L // STRIP), forward, 0)
-    my_y = cols(x, CB)
-    y[:, my_y] = lax.dot_general(perm[...], ypos[...], TN, preferred_element_type=F32).astype(BF16)
-    y_x = send(y.at[:, my_y], y.at[:, my_y], csem, 7, {"ctx": xb})
 
     wy[2].wait_recv()
     wy[3].wait_recv()
@@ -242,6 +264,13 @@
             dysend[rs, :] = there[a * ROWS : (a + 1) * ROWS]
             dypos[rs, :] = here[a * ROWS : (a + 1) * ROWS]
 
+    d_x = []
+
+    def send_grads(zz):
+        for a in range(2):
+            rs = pl.ds(pl.multiple_of(a * 512 + zz * ROWS, ROWS), ROWS)
+            d_x.append(send(dysend.at[rs], dyrecv.at[rs], (d_s, d_r), len(d_x), {"ctx": xb}))
+
     def grads_step(n, carry):
         grads_of(lax.rem(z + 1 + 2 * n, 4))
         return carry
@@ -253,13 +282,17 @@
     d_oth.wait_recv()
     on_u = send(cotz.at[0, zdl], cotz.at[0, zdl], csem, 5, {"ctx": zu})
     on_d = send(cotz.at[1, zul], cotz.at[1, zul], csem, 6, {"ctx": zd})
+    send_grads(z)
     lax.fori_loop(0, 2, grads_step, 0)
+    send_grads(zul)
+    send_grads(zdl)
     on_u.wait_recv()
     on_d.wait_recv()
     grads_of(zo)
-    d_x = send(dysend, dyrecv, csem, 8, {"ctx": xb})
-
-    y_x.wait_recv()
+    send_grads(zo)
+
+    for c in y_x:
+        c.wait_recv()
 
     def part(n, carry):
         def rows_of(b):
@@ -329,7 +362,8 @@
         send(gown.at[yd, 0], ggot2.at[1, 0], vsem, 4, {"dp": dn_y}),
     ]
 
-    d_x.wait_recv()
+    for c in d_x:
+        c.wait_recv()
 
     def add_dy(rs):
         ypos[rs, :] = (dypos[rs, :] + dyrecv[rs, :].astype(F32)).astype(BF16)
@@ -337,13 +371,19 @@
     strips(L, 64, add_dy)
     dypos[pl.ds(0, L), :] = jnp.dot(perm[...], ypos[...], preferred_element_type=F32)
 
-    a_out = []
-    for c in range(2):
+    def out_copy(c, n):
+        p = j if n is None else peer(x, z, *A2A[n])
+        src = arrived.at[:, pl.ds(pl.multiple_of(p * ROWS, ROWS), ROWS), cols(c, 128)]
+        dst = dugot.at[:, :, pl.ds(pl.multiple_of(j * CB + c * 128, 128), 128)]
+        if n is None:
+            return pltpu.make_async_copy(src, dst, l_s.at[4 + c])
+        return remote(src, dst, (q_s, q_r), c * 7 + n, {"ctx": p})
+
+    def chunk(c, carry):
+        cs = cols(c, 128)
 
         def backward(n, carry):
-            h0 = pl.multiple_of(lax.rem(n, 2) * 128, 128)
-            cs = pl.ds(pl.multiple_of(c * 256 + h0, 128), 128)
-            r0 = pl.multiple_of((n // 2) * STRIP, STRIP)
+            r0 = pl.multiple_of(n * STRIP, STRIP)
             m = mask[pl.ds(r0 + PAD, STRIP + 8), :]
             q, k, v, w = [feats[a, pl.ds(r0, STRIP + PAD), cs].astype(F32)[: STRIP + 8] for a in range(4)]
             dy = dypos[pl.ds(r0, STRIP + 8), cs]
@@ -361,7 +401,7 @@
                 gacc[9 + t, :, cs] += total(b[:STRIP] * zs)
             df = (dy * w, dz * v, dz * k)
             for a in range(3):
-                u = upos[pl.ds(PAD + r0, STRIP), pl.ds(pl.multiple_of(a * CB + c * 256 + h0, 128), 128)].astype(F32)
+                u = upos[pl.ds(PAD + r0, STRIP), pl.ds(pl.multiple_of(a * CB + c * 128, 128), 128)].astype(F32)
                 b = df[a]
                 du = short[0, pl.ds(a, 1), cs] * b
                 gacc[a, :, cs] += total(b[:STRIP] * u)
@@ -369,33 +409,30 @@
                     b = up(b, m)
                     du = du + short[t, pl.ds(a, 1), cs] * b
                     gacc[t * 3 + a, :, cs] += total(b[:STRIP] * u)
-                dupos[pl.ds(r0, STRIP), pl.ds(pl.multiple_of(a * 256 + h0, 128), 128)] = du[:STRIP].astype(BF16)
+                dupos[pl.ds(r0, STRIP), pl.ds(a * 128, 128)] = du[:STRIP].astype(BF16)
             return carry
 
-        lax.fori_loop(0, 2 * (L // STRIP), backward, 0)
+        lax.fori_loop(0, L // STRIP, backward, 0)
         val = lax.dot_general(perm[...], dupos[...], TN, preferred_element_type=F32).astype(BF16)
-        part_c = pl.ds(c * 256, 256)
         for a in range(3):
-            arrived[a, :, part_c] = val[:, a * 256 : (a + 1) * 256]
-        there = dugot.at[:, :, pl.ds(pl.multiple_of(j * CB + c * 256, 256), 256)]
-        for n, (dx, dz_) in enumerate(A2A):
-            p = peer(x, z, dx, dz_)
-            rs = pl.ds(pl.multiple_of(p * ROWS, ROWS), ROWS)
-            a_out.append(send(arrived.at[:, rs, part_c], there, (q_s, q_r), c * 7 + n, {"ctx": p}))
-        lc = pltpu.make_async_copy(arrived.at[:, mine_rows, part_c], there, l_s.at[4 + c])
-        lc.start()
-        a_out.append(lc)
-        if c == 0:
-            gy[0].wait_recv()
-            gy[1].wait_recv()
-            for a, k in ((0, yu), (1, yd)):
-
-                def add_fwd(rs):
-                    gfwd[a, rs, :] = (gown[k, a, rs, :].astype(F32) + ggot1[a, rs, :].astype(F32)).astype(BF16)
-
-                strips(256, 64, add_fwd)
-            gy.append(send(gfwd.at[0], ggot2.at[0, 0], vsem, 5, {"dp": up_y}))
-            gy.append(send(gfwd.at[1], ggot2.at[1, 1], vsem, 6, {"dp": dn_y}))
+            arrived[a, :, cs] = val[:, a * 128 : (a + 1) * 128]
+        for n in range(7):
+            out_copy(c, n).start()
+        out_copy(c, None).start()
+        return carry
+
+    lax.fori_loop(0, 2, chunk, 0)
+    gy[0].wait_recv()
+    gy[1].wait_recv()
+    for a, k in ((0, yu), (1, yd)):
+
+        def add_fwd(rs):
+            gfwd[a, rs, :] = (gown[k, a, rs, :].astype(F32) + ggot1[a, rs, :].astype(F32)).astype(BF16)
+
+        strips(256, 64, add_fwd)
+    gy.append(send(gfwd.at[0], ggot2.at[0, 0], vsem, 5, {"dp": up_y}))
+    gy.append(send(gfwd.at[1], ggot2.at[1, 1], vsem, 6, {"dp": dn_y}))
+    lax.fori_loop(2, 4, chunk, 0)
 
     for k in range(16):
         gall[0, pl.ds(k, 1), :] = jnp.sum(gacc[k], axis=0, keepdims=True)
@@ -492,12 +529,13 @@
 
     m_own.wait()
     m_x.wait()
-    for cp in (w_a, *wy, *ws, *a_in, over, u_own, d_own, u_oth, d_oth, on_u, on_d, y_x, d_x):
+    for cp in (w_a, *wy, *ws, *a_in, over, u_own, d_own, u_oth, d_oth, on_u, on_d, *y_x, *d_x):
         cp.wait_send()
     for cp in (s_u, s_d, t_u, t_d, f_u, f_d, g_sib, *gy, *gx):
         cp.wait_send()
-    for cp in a_out:
-        cp.wait()
+    for c in range(4):
+        for n in (*range(7), None):
+            out_copy(c, n).wait()
 
 
 VM = pl.BlockSpec(memory_space=pltpu.VMEM)
@@ -540,7 +578,7 @@
             vm((L, CB), BF16),
             vm((L, CB), BF16),
             vm((L + 8, CB), F32),
-            vm((L, 768), BF16),
+            vm((L, 384), BF16),
             vm((4, 2, ROWS, HF), BF16),
             vm((2, ROWS, HF), BF16),
             vm((2, ROWS, HF), BF16),
@@ -556,8 +594,8 @@
             vm((2, 2, 256, CB), BF16),
             vm((2, 256, CB), BF16),
             vm((2, 256, CB), BF16),
-            *sems(7, 9, 10, 7, 14, 4, 9),
-            DMA((6,)),
+            *sems(14, 9, 10, 7, 28, 4, 9, 8),
+            DMA((9,)),
         ],
         compiler_params=pltpu.CompilerParams(collective_id=0, has_side_effects=True, vmem_limit_bytes=60 << 20),
         cost_estimate=pl.CostEstimate(flops=30 << 30, bytes_accessed=100 << 20, transcendentals=0),

time: 197 us -> 185 us (0.939); the launches traced: 196 us -> 182 us
  Pallas kernels: 187 us -> 173 us
    pallas_call x1, Pallas kernels: 187 us -> 173 us  [block(): pl.pallas_call(block_kernel, out_shape=(sds((ROWS, 2 * HF), BF16), sds((3...]
where the time goes in v1:
time: 185 us; the launch traced here: 182 us
  Pallas kernels  173 us (94%)
  local copies, waits for them, and re-layouts  8.26 us (4%)
    pallas_call x1, Pallas kernels, block(): pl.pallas_call(block_kernel, out_shape=(sds((ROWS, 2 * HF), BF16), sds((3...  173 us
    unnamed x11, local copies, waits for them, and re-layouts  8.26 us

profile of v1, /device:TPU:0, one launch (start us, length us, event | category | flops | bytes accessed | tf_op | source)
XLA Modules:
  0.0 182.3 jit_solution(1881055946115281975)
XLA Ops:
  0.6 173.4 %block.1 = (bf16[128,4096]{1,0:T(8,128)(2,1)}, bf16[3,128,4096]{2,1,0:T(8,128)(2,1)}, f32[256,512]{1,0:T(8,128)}, f32[3,3,512]{2,1,0:T(4,128)}, f32[7,32]{1,0:T(8,128)}) custom-call(bf16[3,128,4096]{2,1,0:T(8,128)(2,1)} %bitcast.3, bf16[128,4096]{1,0:T(8,128)(2,1)} %cot.1, bf16[256,512]{1,0:T(8,128)(2,1)} %wt.1, s32[1,1024]{1,0:T(1,128)} %order_row.1, ...), custom_call_target="tpu_custom_call" | custom-call | flops 32212254720 | bytes 104857600 | tf_op jit(solution)/shard_map/block/pallas_call | solution.py:556
  174.1 2.3 %copy.17 = bf16[128,4096]{1,0:T(8,128)(2,1)} copy(bf16[128,4096]{1,0:T(8,128)(2,1)} %get-tuple-element.20) | data formatting | bytes 2097152
  176.4 0.0 copy-start
  176.4 0.0 copy-start.1
  176.4 0.0 copy-start.2
  176.4 4.0 %copy.18 = bf16[128,3,4096]{2,0,1:T(8,128)(2,1)} copy(bf16[128,3,4096]{2,0,1:T(8,128)(2,1)} %bitcast.2) | data formatting | bytes 6291456
  180.3 0.0 copy-done
  180.3 0.8 copy.19
  181.1 0.0 copy-done.1
  181.1 0.6 copy.20
  181.7 0.0 copy-done.2
  181.7 0.6 copy.21
Async XLA Ops:
  176.4 4.0 %copy-start = (f32[256,512]{1,0:T(8,128)S(1)}, f32[256,512]{1,0:T(8,128)}, u32[]{:S(2)}) copy-start(f32[256,512]{1,0:T(8,128)} %get-tuple-element.22) | copy-start | bytes 1572868
  176.4 4.8 %copy-start.1 = (f32[3,3,512]{2,1,0:T(4,128)S(1)}, f32[3,3,512]{2,1,0:T(4,128)}, u32[]{:S(2)}) copy-start(f32[3,3,512]{2,1,0:T(4,128)} %get-tuple-element.23) | copy-start | bytes 55300
  176.4 5.4 %copy-start.2 = (f32[7,32]{1,0:T(8,128)S(1)}, f32[7,32]{1,0:T(8,128)}, u32[]{:S(2)}) copy-start(f32[7,32]{1,0:T(8,128)} %get-tuple-element.24) | copy-start | bytes 2692

commit v2 on v1

--- a/solution.py
+++ b/solution.py
@@ -282,32 +282,40 @@
     d_oth.wait_recv()
     on_u = send(cotz.at[0, zdl], cotz.at[0, zdl], csem, 5, {"ctx": zu})
     on_d = send(cotz.at[1, zul], cotz.at[1, zul], csem, 6, {"ctx": zd})
-    send_grads(z)
     lax.fori_loop(0, 2, grads_step, 0)
-    send_grads(zul)
-    send_grads(zdl)
+
+    def outputs(blocks, again_):
+        def part(n, carry):
+            val = None
+            for b, c0, width in blocks:
+                term = lax.dot_general(
+                    y[:, pl.ds(pl.multiple_of(b * CB + c0, 256), width)],
+                    w2[b, pl.ds(n * 2, 2), :, pl.ds(c0, width)].reshape(512, width),
+                    NT,
+                    preferred_element_type=F32,
+                )
+                val = term if val is None else val + term
+            for a in range(2):
+                for zz in range(4):
+                    r0 = (a * 4 + zz) * ROWS
+                    place = (lax.rem(zz - z + 4, 4), a, slice(None), cols(n, 512))
+                    rows = val[r0 : r0 + ROWS]
+                    parts[place] = (rows + parts[place].astype(F32) if again_ else rows).astype(BF16)
+            return carry
+
+        lax.fori_loop(0, HF // 512, part, 0)
+
+    y_x[0].wait_recv()
+    outputs(((x, 0, CB), (1 - x, 0, 256)), False)
     on_u.wait_recv()
     on_d.wait_recv()
     grads_of(zo)
-    send_grads(zo)
-
-    for c in y_x:
-        c.wait_recv()
-
-    def part(n, carry):
-        def rows_of(b):
-            return w2[b, pl.ds(n * 2, 2)].reshape(512, CB)
-
-        val = lax.dot_general(y[:, pl.ds(0, CB)], rows_of(0), NT, preferred_element_type=F32) + lax.dot_general(
-            y[:, pl.ds(CB, CB)], rows_of(1), NT, preferred_element_type=F32
-        )
-        for a in range(2):
-            for zz in range(4):
-                r0 = (a * 4 + zz) * ROWS
-                parts[lax.rem(zz - z + 4, 4), a, :, cols(n, 512)] = val[r0 : r0 + ROWS].astype(BF16)
-        return carry
-
-    lax.fori_loop(0, HF // 512, part, 0)
+
+    y_x[1].wait_recv()
+    for k in (zo, z, zul, zdl):
+        send_grads(k)
+    outputs(((1 - x, 256, 256),), True)
+
     rsem = (r_s, r_r)
     s_u = send(parts.at[2, 0], got1.at[0], rsem, 0, {"ctx": zu})
     s_d = send(parts.at[2, 1], got1.at[1], rsem, 1, {"ctx": zd})

time: 185 us -> 188 us (1.016); the launches traced: 182 us -> 188 us
  Pallas kernels: 173 us -> 179 us
    pallas_call x1, Pallas kernels: 173 us -> 179 us  [block(): pl.pallas_call(block_kernel, out_shape=(sds((ROWS, 2 * HF), BF16), sds((3...]
where the time goes in v2:
time: 188 us
  Pallas kernels  179 us (95%)
  local copies, waits for them, and re-layouts  8.26 us (4%)
    pallas_call x1, Pallas kernels, block(): pl.pallas_call(block_kernel, out_shape=(sds((ROWS, 2 * HF), BF16), sds((3...  179 us
    unnamed x11, local copies, waits for them, and re-layouts  8.26 us

profile of v2, /device:TPU:0, one launch (start us, length us, event | category | flops | bytes accessed | tf_op | source)
XLA Modules:
  0.0 187.8 jit_solution(14326607013376445448)
XLA Ops:
  0.6 178.9 %block.1 = (bf16[128,4096]{1,0:T(8,128)(2,1)}, bf16[3,128,4096]{2,1,0:T(8,128)(2,1)}, f32[256,512]{1,0:T(8,128)}, f32[3,3,512]{2,1,0:T(4,128)}, f32[7,32]{1,0:T(8,128)}) custom-call(bf16[3,128,4096]{2,1,0:T(8,128)(2,1)} %bitcast.3, bf16[128,4096]{1,0:T(8,128)(2,1)} %cot.1, bf16[256,512]{1,0:T(8,128)(2,1)} %wt.1, s32[1,1024]{1,0:T(1,128)} %order_row.1, ...), custom_call_target="tpu_custom_call" | custom-call | flops 32212254720 | bytes 104857600 | tf_op jit(solution)/shard_map/block/pallas_call | solution.py:564
  179.5 2.3 %copy.17 = bf16[128,4096]{1,0:T(8,128)(2,1)} copy(bf16[128,4096]{1,0:T(8,128)(2,1)} %get-tuple-element.20) | data formatting | bytes 2097152
  181.8 0.0 copy-start
  181.8 0.0 copy-start.1
  181.8 0.0 copy-start.2
  181.8 4.0 %copy.18 = bf16[128,3,4096]{2,0,1:T(8,128)(2,1)} copy(bf16[128,3,4096]{2,0,1:T(8,128)(2,1)} %bitcast.2) | data formatting | bytes 6291456
  185.8 0.0 copy-done
  185.8 0.8 copy.19
  186.6 0.0 copy-done.1
  186.6 0.6 copy.20
  187.2 0.0 copy-done.2
  187.2 0.6 copy.21
Async XLA Ops:
  181.8 4.0 %copy-start = (f32[256,512]{1,0:T(8,128)S(1)}, f32[256,512]{1,0:T(8,128)}, u32[]{:S(2)}) copy-start(f32[256,512]{1,0:T(8,128)} %get-tuple-element.22) | copy-start | bytes 1572868
  181.8 4.8 %copy-start.1 = (f32[3,3,512]{2,1,0:T(4,128)S(1)}, f32[3,3,512]{2,1,0:T(4,128)}, u32[]{:S(2)}) copy-start(f32[3,3,512]{2,1,0:T(4,128)} %get-tuple-element.23) | copy-start | bytes 55300
  181.8 5.4 %copy-start.2 = (f32[7,32]{1,0:T(8,128)S(1)}, f32[7,32]{1,0:T(8,128)}, u32[]{:S(2)}) copy-start(f32[7,32]{1,0:T(8,128)} %get-tuple-element.24) | copy-start | bytes 2692

commit v3 on v0

--- a/solution.py
+++ b/solution.py
@@ -92,7 +92,7 @@
     dysend, dyrecv, dypos, dupos,
     parts, fwd, got1, got2, final, gacc, gall,
     gsib, ggot, gown, gfwd, ggot1, ggot2, gred, gfin,
-    a_s, a_r, c_s, c_r, w_s, w_r, r_s, r_r, q_s, q_r, g_s, g_r, v_s, v_r, l_s,
+    a_s, a_r, c_s, c_r, w_s, w_r, r_s, r_r, q_s, q_r, g_s, g_r, v_s, v_r, d_s, d_r, l_s,
 ):
     j, x, z = where_am_i()
     i, h, yy, core = coords()
@@ -121,6 +121,20 @@
     def cols(k, width):
         return pl.ds(pl.multiple_of(k * width, width), width)
 
+    wsem = (w_s, w_r)
+    w_mine = w2.at[x, yy * 2 + core]
+    w_a = send(wt, w_mine, wsem, 0, {"dp": flip, "ctx": h * 4 + z}, x)
+    w_b = remote(wt, w_mine, wsem, 1, {"ctx": h * 4 + z}, x)
+    w_l = pltpu.make_async_copy(wt, w_mine, l_s.at[3])
+
+    @pl.when(h != x)
+    def _():
+        w_b.start()
+
+    @pl.when(h == x)
+    def _():
+        w_l.start()
+
     mine_rows = pl.ds(pl.multiple_of(j * ROWS, ROWS), ROWS)
     a_in = []
     for n, (dx, dz) in enumerate(A2A):
@@ -128,20 +142,6 @@
         a_in.append(send(qs.at[:, :, cols(p, CB)], arrived.at[:, mine_rows, :], (a_s, a_r), n, {"ctx": p}))
     own_q = pltpu.make_async_copy(qs.at[:, :, cols(j, CB)], arrived.at[:, mine_rows, :], l_s.at[0])
     own_q.start()
-
-    wsem = (w_s, w_r)
-    w_mine = w2.at[x, yy * 2 + core]
-    w_a = send(wt, w_mine, wsem, 0, {"dp": flip, "ctx": h * 4 + z}, x)
-    w_b = remote(wt, w_mine, wsem, 1, {"ctx": h * 4 + z}, x)
-    w_l = pltpu.make_async_copy(wt, w_mine, l_s.at[3])
-
-    @pl.when(h != x)
-    def _():
-        w_b.start()
-
-    @pl.when(h == x)
-    def _():
-        w_l.start()
 
     mine_c = cot.at[:, cols(x, HF)]
     own_c = pltpu.make_async_copy(mine_c, cotz.at[x, z], l_s.at[1])
@@ -242,6 +242,13 @@
             dysend[rs, :] = there[a * ROWS : (a + 1) * ROWS]
             dypos[rs, :] = here[a * ROWS : (a + 1) * ROWS]
 
+    d_x = []
+
+    def send_grads(zz):
+        for a in range(2):
+            rs = pl.ds(pl.multiple_of(a * 512 + zz * ROWS, ROWS), ROWS)
+            d_x.append(send(dysend.at[rs], dyrecv.at[rs], (d_s, d_r), len(d_x), {"ctx": xb}))
+
     def grads_step(n, carry):
         grads_of(lax.rem(z + 1 + 2 * n, 4))
         return carry
@@ -257,9 +264,10 @@
     on_u.wait_recv()
     on_d.wait_recv()
     grads_of(zo)
-    d_x = send(dysend, dyrecv, csem, 8, {"ctx": xb})
 
     y_x.wait_recv()
+    for k in (z, zul, zdl, zo):
+        send_grads(k)
 
     def part(n, carry):
         def rows_of(b):
@@ -329,7 +337,8 @@
         send(gown.at[yd, 0], ggot2.at[1, 0], vsem, 4, {"dp": dn_y}),
     ]
 
-    d_x.wait_recv()
+    for c in d_x:
+        c.wait_recv()
 
     def add_dy(rs):
         ypos[rs, :] = (dypos[rs, :] + dyrecv[rs, :].astype(F32)).astype(BF16)
@@ -337,13 +346,19 @@
     strips(L, 64, add_dy)
     dypos[pl.ds(0, L), :] = jnp.dot(perm[...], ypos[...], preferred_element_type=F32)
 
-    a_out = []
-    for c in range(2):
+    def out_copy(c, n):
+        p = j if n is None else peer(x, z, *A2A[n])
+        src = arrived.at[:, pl.ds(pl.multiple_of(p * ROWS, ROWS), ROWS), cols(c, 128)]
+        dst = dugot.at[:, :, pl.ds(pl.multiple_of(j * CB + c * 128, 128), 128)]
+        if n is None:
+            return pltpu.make_async_copy(src, dst, l_s.at[4 + c])
+        return remote(src, dst, (q_s, q_r), c * 7 + n, {"ctx": p})
+
+    def chunk(c, carry):
+        cs = cols(c, 128)
 
         def backward(n, carry):
-            h0 = pl.multiple_of(lax.rem(n, 2) * 128, 128)
-            cs = pl.ds(pl.multiple_of(c * 256 + h0, 128), 128)
-            r0 = pl.multiple_of((n // 2) * STRIP, STRIP)
+            r0 = pl.multiple_of(n * STRIP, STRIP)
             m = mask[pl.ds(r0 + PAD, STRIP + 8), :]
             q, k, v, w = [feats[a, pl.ds(r0, STRIP + PAD), cs].astype(F32)[: STRIP + 8] for a in range(4)]
             dy = dypos[pl.ds(r0, STRIP + 8), cs]
@@ -361,7 +376,7 @@
                 gacc[9 + t, :, cs] += total(b[:STRIP] * zs)
             df = (dy * w, dz * v, dz * k)
             for a in range(3):
-                u = upos[pl.ds(PAD + r0, STRIP), pl.ds(pl.multiple_of(a * CB + c * 256 + h0, 128), 128)].astype(F32)
+                u = upos[pl.ds(PAD + r0, STRIP), pl.ds(pl.multiple_of(a * CB + c * 128, 128), 128)].astype(F32)
                 b = df[a]
                 du = short[0, pl.ds(a, 1), cs] * b
                 gacc[a, :, cs] += total(b[:STRIP] * u)
@@ -369,33 +384,30 @@
                     b = up(b, m)
                     du = du + short[t, pl.ds(a, 1), cs] * b
                     gacc[t * 3 + a, :, cs] += total(b[:STRIP] * u)
-                dupos[pl.ds(r0, STRIP), pl.ds(pl.multiple_of(a * 256 + h0, 128), 128)] = du[:STRIP].astype(BF16)
+                dupos[pl.ds(r0, STRIP), pl.ds(a * 128, 128)] = du[:STRIP].astype(BF16)
             return carry
 
-        lax.fori_loop(0, 2 * (L // STRIP), backward, 0)
+        lax.fori_loop(0, L // STRIP, backward, 0)
         val = lax.dot_general(perm[...], dupos[...], TN, preferred_element_type=F32).astype(BF16)
-        part_c = pl.ds(c * 256, 256)
         for a in range(3):
-            arrived[a, :, part_c] = val[:, a * 256 : (a + 1) * 256]
-        there = dugot.at[:, :, pl.ds(pl.multiple_of(j * CB + c * 256, 256), 256)]
-        for n, (dx, dz_) in enumerate(A2A):
-            p = peer(x, z, dx, dz_)
-            rs = pl.ds(pl.multiple_of(p * ROWS, ROWS), ROWS)
-            a_out.append(send(arrived.at[:, rs, part_c], there, (q_s, q_r), c * 7 + n, {"ctx": p}))
-        lc = pltpu.make_async_copy(arrived.at[:, mine_rows, part_c], there, l_s.at[4 + c])
-        lc.start()
-        a_out.append(lc)
-        if c == 0:
-            gy[0].wait_recv()
-            gy[1].wait_recv()
-            for a, k in ((0, yu), (1, yd)):
-
-                def add_fwd(rs):
-                    gfwd[a, rs, :] = (gown[k, a, rs, :].astype(F32) + ggot1[a, rs, :].astype(F32)).astype(BF16)
-
-                strips(256, 64, add_fwd)
-            gy.append(send(gfwd.at[0], ggot2.at[0, 0], vsem, 5, {"dp": up_y}))
-            gy.append(send(gfwd.at[1], ggot2.at[1, 1], vsem, 6, {"dp": dn_y}))
+            arrived[a, :, cs] = val[:, a * 128 : (a + 1) * 128]
+        for n in range(7):
+            out_copy(c, n).start()
+        out_copy(c, None).start()
+        return carry
+
+    lax.fori_loop(0, 2, chunk, 0)
+    gy[0].wait_recv()
+    gy[1].wait_recv()
+    for a, k in ((0, yu), (1, yd)):
+
+        def add_fwd(rs):
+            gfwd[a, rs, :] = (gown[k, a, rs, :].astype(F32) + ggot1[a, rs, :].astype(F32)).astype(BF16)
+
+        strips(256, 64, add_fwd)
+    gy.append(send(gfwd.at[0], ggot2.at[0, 0], vsem, 5, {"dp": up_y}))
+    gy.append(send(gfwd.at[1], ggot2.at[1, 1], vsem, 6, {"dp": dn_y}))
+    lax.fori_loop(2, 4, chunk, 0)
 
     for k in range(16):
         gall[0, pl.ds(k, 1), :] = jnp.sum(gacc[k], axis=0, keepdims=True)
@@ -492,12 +504,13 @@
 
     m_own.wait()
     m_x.wait()
-    for cp in (w_a, *wy, *ws, *a_in, over, u_own, d_own, u_oth, d_oth, on_u, on_d, y_x, d_x):
+    for cp in (w_a, *wy, *ws, *a_in, over, u_own, d_own, u_oth, d_oth, on_u, on_d, y_x, *d_x):
         cp.wait_send()
     for cp in (s_u, s_d, t_u, t_d, f_u, f_d, g_sib, *gy, *gx):
         cp.wait_send()
-    for cp in a_out:
-        cp.wait()
+    for c in range(4):
+        for n in (*range(7), None):
+            out_copy(c, n).wait()
 
 
 VM = pl.BlockSpec(memory_space=pltpu.VMEM)
@@ -540,7 +553,7 @@
             vm((L, CB), BF16),
             vm((L, CB), BF16),
             vm((L + 8, CB), F32),
-            vm((L, 768), BF16),
+            vm((L, 384), BF16),
             vm((4, 2, ROWS, HF), BF16),
             vm((2, ROWS, HF), BF16),
             vm((2, ROWS, HF), BF16),
@@ -556,8 +569,8 @@
             vm((2, 2, 256, CB), BF16),
             vm((2, 256, CB), BF16),
             vm((2, 256, CB), BF16),
-            *sems(7, 9, 10, 7, 14, 4, 9),
-            DMA((6,)),
+            *sems(7, 8, 10, 7, 28, 4, 9, 8),
+            DMA((8,)),
         ],
         compiler_params=pltpu.CompilerParams(collective_id=0, has_side_effects=True, vmem_limit_bytes=60 << 20),
         cost_estimate=pl.CostEstimate(flops=30 << 30, bytes_accessed=100 << 20, transcendentals=0),

time: 197 us -> 181 us (0.919)
  Pallas kernels: 187 us -> 171 us
    pallas_call x1, Pallas kernels: 187 us -> 171 us  [block(): pl.pallas_call(block_kernel, out_shape=(sds((ROWS, 2 * HF), BF16), sds((3...]
where the time goes in v3:
time: 181 us; the launch traced here: 180 us
  Pallas kernels  171 us (94%)
  local copies, waits for them, and re-layouts  8.26 us (5%)
    pallas_call x1, Pallas kernels, block(): pl.pallas_call(block_kernel, out_shape=(sds((ROWS, 2 * HF), BF16), sds((3...  171 us
    unnamed x11, local copies, waits for them, and re-layouts  8.26 us

profile of v3, /device:TPU:0, one launch (start us, length us, event | category | flops | bytes accessed | tf_op | source)
XLA Modules:
  0.0 180.3 jit_solution(17195003739917470808)
XLA Ops:
  0.6 171.4 %block.1 = (bf16[128,4096]{1,0:T(8,128)(2,1)}, bf16[3,128,4096]{2,1,0:T(8,128)(2,1)}, f32[256,512]{1,0:T(8,128)}, f32[3,3,512]{2,1,0:T(4,128)}, f32[7,32]{1,0:T(8,128)}) custom-call(bf16[3,128,4096]{2,1,0:T(8,128)(2,1)} %bitcast.3, bf16[128,4096]{1,0:T(8,128)(2,1)} %cot.1, bf16[256,512]{1,0:T(8,128)(2,1)} %wt.1, s32[1,1024]{1,0:T(1,128)} %order_row.1, ...), custom_call_target="tpu_custom_call" | custom-call | flops 32212254720 | bytes 104857600 | tf_op jit(solution)/shard_map/block/pallas_call | solution.py:531
  172.0 2.3 %copy.17 = bf16[128,4096]{1,0:T(8,128)(2,1)} copy(bf16[128,4096]{1,0:T(8,128)(2,1)} %get-tuple-element.20) | data formatting | bytes 2097152
  174.3 0.0 copy-start
  174.3 0.0 copy-start.1
  174.3 0.0 copy-start.2
  174.3 4.0 %copy.18 = bf16[128,3,4096]{2,0,1:T(8,128)(2,1)} copy(bf16[128,3,4096]{2,0,1:T(8,128)(2,1)} %bitcast.2) | data formatting | bytes 6291456
  178.3 0.0 copy-done
  178.3 0.8 copy.19
  179.1 0.0 copy-done.1
  179.1 0.6 copy.20
  179.7 0.0 copy-done.2
  179.7 0.6 copy.21
Async XLA Ops:
  174.3 4.0 %copy-start = (f32[256,512]{1,0:T(8,128)S(1)}, f32[256,512]{1,0:T(8,128)}, u32[]{:S(2)}) copy-start(f32[256,512]{1,0:T(8,128)} %get-tuple-element.22) | copy-start | bytes 1572868
  174.3 4.8 %copy-start.1 = (f32[3,3,512]{2,1,0:T(4,128)S(1)}, f32[3,3,512]{2,1,0:T(4,128)}, u32[]{:S(2)}) copy-start(f32[3,3,512]{2,1,0:T(4,128)} %get-tuple-element.23) | copy-start | bytes 55300
  174.3 5.4 %copy-start.2 = (f32[7,32]{1,0:T(8,128)S(1)}, f32[7,32]{1,0:T(8,128)}, u32[]{:S(2)}) copy-start(f32[7,32]{1,0:T(8,128)} %get-tuple-element.24) | copy-start | bytes 2692
